TPU v7x, 256 devices: a whole 4x4x8 slice. The times are simulated.
256 devices in a mesh: slide: 8 (over z), tile: 32 (over y, x, core).
Axes of the slice: x: 4, y: 4, z: 8, core: 2. Of those that a mesh axis runs over, the one named last changes fastest.
Arguments:
- features: bfloat16 [8, 448, 98, 384], P('slide', 'tile'), may hold values from -6 to 6
- cotangent: bfloat16 [8, 448, 98, 384], P('slide', 'tile'), may hold values from -6 to 6
- owner_slot: int32 [8, 64, 14], P('slide'), may hold values from -1 to 511, as said below
- dw_weight: float32 [7, 7, 384], replicated, may hold values from -0.875 to 0.875
- dw_bias: float32 [384], replicated, may hold values from -3 to 3
- ln_gain: float32 [384], replicated, may hold values from 0.1 to 1.9
- ln_bias: float32 [384], replicated, may hold values from -3 to 3
- w_in: bfloat16 [384, 1536], replicated, may hold values from -0.3125 to 0.3125
- b_in: float32 [1536], replicated, may hold values from -3 to 3
- w_out: bfloat16 [1536, 384], replicated, may hold values from -0.15625 to 0.15625
- b_out: float32 [384], replicated, may hold values from -3 to 3
- layer_scale: float32 [384], replicated, may hold values from 0.25 to 1
Outputs:
- mixed: bfloat16 [8, 448, 98, 384], P('slide', 'tile')
- grad_dw_weight: float32 [7, 7, 384], replicated
- grad_dw_bias: float32 [384], replicated
- grad_ln_gain: float32 [384], replicated
- grad_ln_bias: float32 [384], replicated
- grad_w_in: float32 [384, 1536], replicated
- grad_b_in: float32 [1536], replicated
- grad_w_out: float32 [1536, 384], replicated
- grad_b_out: float32 [384], replicated
- grad_layer_scale: float32 [384], replicated
Inputs may be any that keep to these rules, and one draw needn't show every extreme that they name: `owner_slot`: -1 marks a background tile; every other value o names owner device o // 16; each value 0 to 511 appears exactly once in each slide, so every owner device holds 16 tissue tiles. Of the tissue tiles in the 2 rows of one device, at most 1 goes to any one owner device, and for some pair of sender and owner exactly 1 does. In each slide the 2 rows of one device are tissue in all 14 columns.
All inputs are finite; a program needn't handle non-finite values.
Results may differ from a plain program's by a relative error of at most 0.0071.
Values may be sent and summed in bfloat16 or wider, within the bound.
A program may use at most 128 MiB of HBM per device.

v0:
```python
import math

import jax
import jax.numpy as jnp
from jax import lax
from jax.sharding import PartitionSpec as P

C = 384
K = 7
TP = 7
COLS = 14
OWN = 16


def with_halo(block, sides, width):
    for axis, dim in sides:
        count = lax.axis_size(axis)
        forward = [(i, i + 1) for i in range(count - 1)]
        backward = [(target, source) for source, target in forward]
        low = lax.ppermute(
            lax.slice_in_dim(block, block.shape[dim] - width, None, axis=dim), axis, forward
        )
        high = lax.ppermute(lax.slice_in_dim(block, 0, width, axis=dim), axis, backward)
        block = jnp.concatenate([low, block, high], axis=dim)
    return block


def gelu_parts(pre_act):
    prob_mass = 0.5 * (1.0 + jax.scipy.special.erf(pre_act * 0.7071067811865476))
    density = jnp.exp(-0.5 * pre_act * pre_act) * 0.3989422804014327
    return (pre_act * prob_mass, prob_mass + pre_act * density)


def depthwise(padded, weight, offset, height, breadth):
    summed = jnp.zeros((height, breadth, padded.shape[2]), jnp.float32) + offset
    for row_tap in range(K):
        for col_tap in range(K):
            summed = (
                summed
                + padded[row_tap : row_tap + height, col_tap : col_tap + breadth, :].astype(
                    jnp.float32
                )
                * weight[row_tap, col_tap]
            )
    return summed


def conv_grad(padded, grad_conv, height, breadth):
    pieces = []
    for row_tap in range(K):
        for col_tap in range(K):
            window = padded[row_tap : row_tap + height, col_tap : col_tap + breadth, :].astype(
                jnp.float32
            )
            pieces.append(jnp.sum(window * grad_conv, axis=(0, 1)))
    return jnp.stack(pieces).reshape(K, K, -1)


def normalize(conv_out, ln_gain, ln_bias):
    mean_val = jnp.mean(conv_out, axis=-1, keepdims=True)
    shifted = conv_out - mean_val
    var_val = jnp.mean(shifted * shifted, axis=-1, keepdims=True)
    inv_std = lax.rsqrt(var_val + 1e-06)
    centred = shifted * inv_std
    return (centred, inv_std, centred * ln_gain + ln_bias)


def contract_rows(left, right):
    return lax.dot_general(
        left, right, (((0,), (0,)), ((), ())), preferred_element_type=jnp.float32
    )


def contract_cols(left, right):
    return lax.dot_general(
        left, right, (((1,), (1,)), ((), ())), preferred_element_type=jnp.float32
    )


def mlp_block(normed, cot_rows, live_rows, w_in, b_in, w_out, b_out, layer_scale, loss_scale):
    pre_act = jnp.dot(normed, w_in, preferred_element_type=jnp.float32) + b_in
    activ, slope = gelu_parts(pre_act)
    hidden = activ.astype(jnp.bfloat16)
    branch = (jnp.dot(hidden, w_out, preferred_element_type=jnp.float32) + b_out).astype(
        jnp.bfloat16
    )
    grad_branch = loss_scale * layer_scale * cot_rows.astype(jnp.float32) * live_rows
    grad_branch_b = grad_branch.astype(jnp.bfloat16)
    grad_b_out = jnp.sum(grad_branch, axis=0)
    grad_w_out = contract_rows(hidden, grad_branch_b)
    grad_pre = contract_cols(grad_branch_b, w_out) * slope
    grad_pre_b = grad_pre.astype(jnp.bfloat16)
    grad_b_in = jnp.sum(grad_pre, axis=0)
    grad_w_in = contract_rows(normed, grad_pre_b)
    grad_xn = contract_cols(grad_pre_b, w_in).astype(jnp.bfloat16)
    return (branch, grad_xn, (grad_w_in, grad_b_in, grad_w_out, grad_b_out))


def local(
    features,
    cotangent,
    owner_slot,
    dw_weight,
    dw_bias,
    ln_gain,
    ln_bias,
    w_in,
    b_in,
    w_out,
    b_out,
    layer_scale,
):
    reach = K // 2
    ntile = lax.axis_size("tile")
    nslide = lax.axis_size("slide")
    loss_scale = 1.0 / math.sqrt(nslide * OWN * ntile * TP * TP)
    my_index = lax.axis_index("tile")
    breadth = COLS * TP
    height = features.shape[1]
    rows_here = height // TP
    tiles_here = rows_here * COLS
    table = owner_slot[0]
    mine = lax.dynamic_slice_in_dim(table, my_index * rows_here, rows_here, 0)
    my_live = mine >= 0
    tile_mask = my_live.astype(jnp.float32)
    tissue = jnp.repeat(jnp.repeat(tile_mask, TP, axis=0), TP, axis=1)[:, :, None]
    slide_feat = features[0]
    slide_cot = cotangent[0]
    masked = slide_feat * tissue.astype(jnp.bfloat16)
    grown = with_halo(masked, (("tile", 0),), reach)
    padded = jnp.pad(grown, ((0, 0), (reach, reach), (0, 0)))
    conv_out = depthwise(padded, dw_weight, dw_bias, height, breadth)
    centred, inv_std, normed_f = normalize(conv_out, ln_gain, ln_bias)
    normed = normed_f.astype(jnp.bfloat16)
    cap = (tiles_here + ntile - 1) // ntile
    slots_all = ntile * cap
    target_dev = jnp.where(table >= 0, table // OWN, -1).reshape(ntile, tiles_here)
    tile_ids = jnp.arange(tiles_here)
    earlier = tile_ids[:, None] < tile_ids[None, :]
    same_dev = target_dev[:, :, None] == target_dev[:, None, :]
    order_in = jnp.sum((same_dev & earlier[None, :, :]).astype(jnp.int32), axis=1)
    buffer_pos = target_dev * cap + order_in
    my_pos = lax.dynamic_slice_in_dim(buffer_pos, my_index, 1, 0)[0]
    buffer_ids = jnp.arange(slots_all)
    flat_live = my_live.reshape(-1)
    send_sel = (
        ((buffer_ids[:, None] == my_pos[None, :]) & flat_live[None, :])
        .astype(jnp.bfloat16)
        .reshape(slots_all, rows_here, COLS)
    )
    send_feat = jnp.einsum(
        "qrc,rpcvk->qpvk",
        send_sel,
        normed.reshape(rows_here, TP, COLS, TP, C),
        preferred_element_type=jnp.bfloat16,
    )
    send_cot = jnp.einsum(
        "qrc,rpcvk->qpvk",
        send_sel,
        slide_cot.reshape(rows_here, TP, COLS, TP, C),
        preferred_element_type=jnp.bfloat16,
    )
    got_feat, got_cot = (
        lax.all_to_all(send_feat, "tile", split_axis=0, concat_axis=0, tiled=True),
        lax.all_to_all(send_cot, "tile", split_axis=0, concat_axis=0, tiled=True),
    )
    source_pos = jnp.arange(ntile)[:, None] * cap + order_in
    for_me = (target_dev == my_index).reshape(-1, 1)
    slot_hot = ((table.reshape(-1) % OWN)[:, None] == jnp.arange(OWN)[None, :]) & for_me
    pos_hot = (source_pos.reshape(-1, 1) == buffer_ids[None, :]) & for_me
    placing = contract_rows(slot_hot.astype(jnp.float32), pos_hot.astype(jnp.float32)).astype(
        jnp.bfloat16
    )
    owned_feat = jnp.einsum(
        "sq,qpvk->spvk", placing, got_feat, preferred_element_type=jnp.bfloat16
    ).reshape(OWN * TP * TP, C)
    owned_cot = jnp.einsum(
        "sq,qpvk->spvk", placing, got_cot, preferred_element_type=jnp.bfloat16
    ).reshape(OWN * TP * TP, C)
    branch_rows, grad_rows, weight_grads = mlp_block(
        owned_feat, owned_cot, 1.0, w_in, b_in, w_out, b_out, layer_scale, loss_scale
    )
    back_branch = jnp.einsum(
        "sq,spvk->qpvk",
        placing,
        branch_rows.reshape(OWN, TP, TP, C),
        preferred_element_type=jnp.bfloat16,
    )
    back_grad = jnp.einsum(
        "sq,spvk->qpvk",
        placing,
        grad_rows.reshape(OWN, TP, TP, C),
        preferred_element_type=jnp.bfloat16,
    )
    ret_branch, ret_grad = (
        lax.all_to_all(back_branch, "tile", split_axis=0, concat_axis=0, tiled=True),
        lax.all_to_all(back_grad, "tile", split_axis=0, concat_axis=0, tiled=True),
    )
    branch = jnp.einsum(
        "qrc,qpvk->rpcvk", send_sel, ret_branch, preferred_element_type=jnp.bfloat16
    ).reshape(height, breadth, C)
    grad_xn = jnp.einsum(
        "qrc,qpvk->rpcvk", send_sel, ret_grad, preferred_element_type=jnp.bfloat16
    ).reshape(height, breadth, C)
    branch_f = branch.astype(jnp.float32)
    grad_xf = grad_xn.astype(jnp.float32)
    mixed = (tissue * (slide_feat.astype(jnp.float32) + layer_scale * branch_f)).astype(
        jnp.bfloat16
    )
    grad_scale = loss_scale * jnp.sum(
        tissue * slide_cot.astype(jnp.float32) * branch_f, axis=(0, 1)
    )
    grad_gain = jnp.sum(grad_xf * centred, axis=(0, 1))
    grad_lnb = jnp.sum(grad_xf, axis=(0, 1))
    scaled = grad_xf * ln_gain
    grad_conv = inv_std * (
        scaled
        - jnp.mean(scaled, axis=-1, keepdims=True)
        - centred * jnp.mean(scaled * centred, axis=-1, keepdims=True)
    )
    grad_dwb = jnp.sum(grad_conv, axis=(0, 1))
    grad_dw = conv_grad(padded, grad_conv, height, breadth)
    grad_w1, grad_b1, grad_w2, grad_b2 = weight_grads
    summed = lax.psum(
        (grad_dw, grad_dwb, grad_gain, grad_lnb, grad_w1, grad_b1, grad_w2, grad_b2, grad_scale),
        ("slide", "tile"),
    )
    return (
        mixed[None],
        summed[0],
        summed[1],
        summed[2],
        summed[3],
        summed[4],
        summed[5],
        summed[6],
        summed[7],
        summed[8],
    )


def solution(mesh):
    placed = (
        P("slide", "tile", None, None),
        P("slide", "tile", None, None),
        P("slide", None, None),
        P(),
        P(),
        P(),
        P(),
        P(),
        P(),
        P(),
        P(),
        P(),
    )
    return jax.shard_map(
        local,
        mesh=mesh,
        in_specs=placed,
        out_specs=(P("slide", "tile", None, None), P(), P(), P(), P(), P(), P(), P(), P(), P()),
        check_vma=False,
    )
```

profile of v0, /device:TPU:1, one launch (start us, length us, event | category | flops | bytes accessed | tf_op | source)
XLA Modules:
  0.0 455.9 jit_solution(13625623467022604869)
XLA Ops:
  7.2 0.9 copy.86
  8.1 0.5 fusion.159
  8.9 1.5 bitcast_multiply_fusion
  10.4 1.0 copy-done.4
  11.4 0.8 fusion.160
  12.2 4.5 collective-permute-start
  16.8 2.6 collective-permute-start.1
  19.8 0.6 copy-done.17
  20.4 0.6 eq.76
  21.4 1.3 convolution_bitcast_fusion
  22.7 1.6 copy.102
  24.2 7.1 %all-to-all-start.2 = ((bf16[32,7,7,384]{3,2,1,0:T(8,128)(2,1)}), bf16[32,7,7,384]{3,2,1,0:T(8,128)(2,1)}, u32[]{:S(2)}, u32[]{:S(2)}) async-start(bf16[32,7,7,384]{3,2,1,0:T(8,128)(2,1)} %copy.102), calls=%async_computation.2 | async-start | bytes 2752512 | tf_op jit(solution)/shard_map/all_to_all | solution.py:165
  31.7 2.1 fusion.111
  33.8 19.8 %fusion.157 = (f32[14,98]{1,0:T(8,128)S(1)}, f32[14,98,384]{2,1,0:T(8,128)S(1)}) fusion(f32[384]{0:T(512)S(1)} %get-tuple-element.114, bf16[20,104,384]{2,1,0:T(8,128)(2,1)S(1)} %fusion.111, f32[384]{0:T(512)S(1)} %get-tuple-element.115, f32[384]{0:T(512)S(1)} %get-tuple-element.68, f32[384]{0:T(512)S(1)} %get-tuple-element.69, ...), kind=kLoop, calls=%fused_computation.360 | loop fusion | flops 81133216 | bytes 47950192 | tf_op jit(solution)/shard_map/reduce_sum | solution.py:60
  53.6 0.5 multiply_reduce_fusion.2
  54.2 0.8 copy-done.2
  55.0 1.5 add_convert_fusion
  56.5 2.2 reshape.281
  58.7 1.9 convolution_bitcast_fusion.1
  60.6 1.6 copy.94
  62.2 7.6 %all-to-all-start = ((bf16[32,7,7,384]{3,2,1,0:T(8,128)(2,1)}), bf16[32,7,7,384]{3,2,1,0:T(8,128)(2,1)}, u32[]{:S(2)}, u32[]{:S(2)}) async-start(bf16[32,7,7,384]{3,2,1,0:T(8,128)(2,1)} %copy.94), calls=%async_computation | async-start | bytes 2752512 | tf_op jit(solution)/shard_map/all_to_all | solution.py:164
  70.1 0.8 fusion.128
  70.9 2.3 multiply_reduce_fusion.3
  73.1 1.5 copy.104
  74.6 2.5 reshape.287
  77.1 12.6 %all-to-all-done = bf16[32,7,7,384]{3,2,1,0:T(8,128)(2,1)} async-done(((bf16[32,7,7,384]{3,2,1,0:T(8,128)(2,1)}), bf16[32,7,7,384]{3,2,1,0:T(8,128)(2,1)}, u32[]{:S(2)}, u32[]{:S(2)}) %all-to-all-start) | async-done | bytes 1204256 | tf_op jit(solution)/shard_map/all_to_all | solution.py:164
  89.7 1.6 fusion.118
  91.5 1.0 reshape.282
  92.6 4.6 %multiply_convert_fusion = (bf16[784,1536]{1,0:T(8,128)(2,1)}, f32[784,1536]{1,0:T(8,128)S(1)}) fusion(f32[1536]{0:T(1024)S(1)} %copy-done.34, bf16[784,384]{1,0:T(8,128)(2,1)} %reshape.282, bf16[384,1536]{1,0:T(8,128)(2,1)S(1)} %copy-done), kind=kOutput, calls=%fused_computation.6 | convolution fusion | flops 932069376 | bytes 9013248 | tf_op jit(solution)/shard_map/dot_general | solution.py:81
  97.2 3.7 fusion.161
  100.9 1.4 copy-done.10
  102.3 1.4 convolution_convert_fusion
  104.4 1.6 copy.106
  106.1 6.2 %all-to-all-start.3 = ((bf16[32,7,7,384]{3,2,1,0:T(8,128)(2,1)}), bf16[32,7,7,384]{3,2,1,0:T(8,128)(2,1)}, u32[]{:S(2)}, u32[]{:S(2)}) async-start(bf16[32,7,7,384]{3,2,1,0:T(8,128)(2,1)} %copy.106), calls=%async_computation.3 | async-start | bytes 2752512 | tf_op jit(solution)/shard_map/all_to_all | solution.py:197
  112.3 4.3 fusion.112
  116.6 1.3 reshape.283
  118.0 4.6 %fusion.121 = f32[384,1536]{1,0:T(8,128)} fusion(bf16[784,384]{1,0:T(8,128)(2,1)S(1)} %copy-done.11, bf16[784,1536]{1,0:T(8,128)(2,1)} %copy-done.10), kind=kOutput, calls=%fused_computation.250 | convolution fusion | flops 924844032 | bytes 5369856 | tf_op jit(solution)/shard_map/dot_general | solution.py:69
  122.6 3.2 fusion.141
  125.8 6.5 %all-to-all-done.3 = bf16[32,7,7,384]{3,2,1,0:T(8,128)(2,1)} async-done(((bf16[32,7,7,384]{3,2,1,0:T(8,128)(2,1)}), bf16[32,7,7,384]{3,2,1,0:T(8,128)(2,1)}, u32[]{:S(2)}, u32[]{:S(2)}) %all-to-all-start.3) | async-done | bytes 1204256 | tf_op jit(solution)/shard_map/all_to_all | solution.py:197
  132.3 3.6 convert_reduce_fusion
  136.3 1.6 convert_bitcast_fusion
  137.8 2.7 copy.108
  140.5 2.8 reshape.288
  143.3 3.3 multiply_reduce_fusion
  147.0 6.4 %fusion.104 = (f32[384]{0:T(512)S(1)}, f32[384]{0:T(512)S(1)}, f32[384]{0:T(512)S(1)}, f32[384]{0:T(512)S(1)}, f32[384]{0:T(512)S(1)}, /*index=5*/f32[384]{0:T(5...) fusion(bf16[20,104,384]{2,1,0:T(8,128)(2,1)S(1)} %fusion.111, ...), kind=kLoop, calls=%fused_computation.211 | loop fusion | flops 32130816 | bytes 25339840 | tf_op jit(solution)/shard_map/reduce_sum | solution.py:55
  153.4 1.8 fusion.38
  155.2 5.5 %fusion.83 = (f32[384]{0:T(512)S(1)}, f32[384]{0:T(512)S(1)}, f32[384]{0:T(512)S(1)}, f32[384]{0:T(512)S(1)}, f32[384]{0:T(512)S(1)}, /*index=5*/f32[384]{0:T(51...) fusion(f32[14,98,384]{2,1,0:T(8,128)S(1)} %get-tuple-element.12, ...), kind=kLoop, calls=%fused_computation.190 | loop fusion | flops 28442880 | bytes 21101568 | tf_op jit(solution)/shard_map/reduce_sum | solution.py:55
  160.7 3.1 fusion.101
  164.5 0.7 reshape.285
  165.2 0.5 fusion.131
  165.7 1.6 copy.98
  167.3 5.6 %all-to-all-start.1 = ((bf16[32,7,7,384]{3,2,1,0:T(8,128)(2,1)}), bf16[32,7,7,384]{3,2,1,0:T(8,128)(2,1)S(1)}, u32[]{:S(2)}, u32[]{:S(2)}) async-start(bf16[32,7,7,384]{3,2,1,0:T(8,128)(2,1)} %copy.98), calls=%async_computation.1 | async-start | bytes 2752512 | tf_op jit(solution)/shard_map/all_to_all | solution.py:196
  173.0 21.4 %all-to-all-done.1 = bf16[32,7,7,384]{3,2,1,0:T(8,128)(2,1)S(1)} async-done(((bf16[32,7,7,384]{3,2,1,0:T(8,128)(2,1)}), bf16[32,7,7,384]{3,2,1,0:T(8,128)(2,1)S(1)}, u32[]{:S(2)}, u32[]{:S(2)}) %all-to-all-start.1) | async-done | bytes 1204256 | tf_op jit(solution)/shard_map/all_to_all | solution.py:196
  194.4 0.5 convert_bitcast_fusion.1
  194.9 2.7 copy.100
  197.6 2.9 reshape.290
  200.5 1.8 reshape.286
  202.4 2.4 fusion.106
  204.9 80.2 %all-reduce.1 = (f32[384]{0:T(512)}, f32[384]{0:T(512)}, f32[384]{0:T(512)}, f32[1536]{0:T(1024)}, f32[384]{0:T(512)}, /*index=5*/f32[384]{0:T(512)}) all-reduce(f32[384]{0:T(512)S(1)} %get-tuple-element.64, f32[384]{0:T(512)S(1)} %get-tuple-element.10, ...), channel_id=1, replica_groups=mesh['slide'=8,'tile'=32] {'slide','tile'}, use_global_device_ids=true, to_apply=%region_56.57 | all-reduce | flops 3456 | bytes 27648 | tf_op jit(solution)/shard_map/psum | solution.py:224
  285.1 1.4 multiply_convert_fusion.1
  286.5 156.3 %all-reduce.5.cloned.1.call-done = (f32[7,7,384]{2,1,0:T(8,128)}, f32[384,1536]{1,0:T(8,128)}, f32[1536,384]{1,0:T(8,128)}) async-done(((f32[7,7,384]{2,1,0:T(8,128)}, f32[384,1536]{1,0:T(8,128)}, f32[1536,384]{1,0:T(8,128)}), (f32[7,7,384]{2,1,0:T(8,128)}, f32[384,1536]{1,0:T(8,128)}, f32[1536,384]{1,0:T(8,128)})) %all-reduce.5.cloned.1.call-update) | async-done | bytes 4793872 | tf_op jit(solution)/shard_map/psum | solution.py:224
  442.8 1.5 copy.145
  444.3 3.4 copy.146
  447.7 1.4 copy.147
  (159 shorter events, 3.6 us)
Async XLA Ops:
  7.2 85.4 %copy-start = (bf16[384,1536]{1,0:T(8,128)(2,1)S(1)}, bf16[384,1536]{1,0:T(8,128)(2,1)}, u32[]{:S(2)}) copy-start(bf16[384,1536]{1,0:T(8,128)(2,1)} %param.19) | copy-start | bytes 3538948
  7.2 13.8 %copy-start.9 = (bf16[1,14,98,384]{3,2,1,0:T(8,128)(2,1)S(1)}, bf16[1,14,98,384]{3,2,1,0:T(8,128)(2,1)}, u32[]{:S(2)}) copy-start(bf16[1,14,98,384]{3,2,1,0:T(8,128)(2,1)} %param.13) | copy-start | bytes 3161092
  8.1 11.7 %copy-start.15 = (s32[1,64,14]{2,1,0:T(8,128)}, s32[1,64,14]{2,1,0:T(8,128)S(1)}, u32[]{:S(2)}) copy-start(s32[1,64,14]{2,1,0:T(8,128)S(1)} %copy.86) | copy-start | bytes 10756
  10.4 1.0 copy-start.4
  12.2 19.4 %collective-permute-start = (bf16[3,98,384]{2,1,0:T(8,128)(2,1)}, bf16[3,98,384]{2,1,0:T(8,128)(2,1)}, u32[]{:S(2)}, u32[]{:S(2)}) collective-permute-start(bf16[3,98,384]{2,1,0:T(8,128)(2,1)} %get-tuple-element.130), channel_id=1, source_target_pairs={{0,1},{1,2},{2,3},{3,4},{4,5},{5,6},{6,7},{7,8},{8,9},{9,10},{10,1... | collective-permute-start | bytes 677384 | tf_op jit(solution)/shard_map/ppermute | solution.py:20
  16.8 14.9 %collective-permute-start.1 = (bf16[3,98,384]{2,1,0:T(8,128)(2,1)}, bf16[3,98,384]{2,1,0:T(8,128)(2,1)}, u32[]{:S(2)}, u32[]{:S(2)}) collective-permute-start(bf16[3,98,384]{2,1,0:T(8,128)(2,1)} %get-tuple-element.131), channel_id=1, source_target_pairs={{1,0},{2,1},{3,2},{4,3},{5,4},{6,5},{7,6},{8,7},{9,8},{10,9},{11,1... | collective-permute-start | bytes 677384 | tf_op jit(solution)/shard_map/ppermute | solution.py:23
  19.8 0.6 copy-start.17
  22.7 8.7 %copy-start.19 = (f32[7,7,384]{2,1,0:T(8,128)S(1)}, f32[7,7,384]{2,1,0:T(8,128)}, u32[]{:S(2)}) copy-start(f32[7,7,384]{2,1,0:T(8,128)} %param.15) | copy-start | bytes 225796
  24.2 37.9 %all-to-all-start.2 = ((bf16[32,7,7,384]{3,2,1,0:T(8,128)(2,1)}), bf16[32,7,7,384]{3,2,1,0:T(8,128)(2,1)}, u32[]{:S(2)}, u32[]{:S(2)}) async-start(bf16[32,7,7,384]{3,2,1,0:T(8,128)(2,1)} %copy.102), calls=%async_computation.2 | async-start | bytes 2752512 | tf_op jit(solution)/shard_map/all_to_all | solution.py:165
  31.3 2.4 copy-start.5
  31.4 2.4 copy-start.30
  53.5 1.4 copy-start.2
  53.6 1.4 copy-start.20
  53.6 1.4 copy-start.31
  55.0 3.7 copy-start.22
  55.0 3.7 copy-start.24
  60.6 9.2 %copy-start.18 = (s32[32,28]{1,0:T(8,128)S(1)}, s32[32,28]{1,0:T(8,128)}, u32[]{:S(2)}) copy-start(s32[32,28]{1,0:T(8,128)} %copy-done.17) | copy-start | bytes 10756
  60.6 9.2 %copy-start.16 = (s32[1,64,14]{2,1,0:T(8,128)S(1)}, s32[1,64,14]{2,1,0:T(8,128)}, u32[]{:S(2)}) copy-start(s32[1,64,14]{2,1,0:T(8,128)} %copy-done.15) | copy-start | bytes 10756
  62.2 8.7 %copy-start.27 = (f32[384]{0:T(512)S(1)}, f32[384]{0:T(512)}, u32[]{:S(2)}) copy-start(f32[384]{0:T(512)} %param.23) | copy-start | bytes 4612
  62.2 27.6 %all-to-all-start = ((bf16[32,7,7,384]{3,2,1,0:T(8,128)(2,1)}), bf16[32,7,7,384]{3,2,1,0:T(8,128)(2,1)}, u32[]{:S(2)}, u32[]{:S(2)}) async-start(bf16[32,7,7,384]{3,2,1,0:T(8,128)(2,1)} %copy.94), calls=%async_computation | async-start | bytes 2752512 | tf_op jit(solution)/shard_map/all_to_all | solution.py:164
  77.1 15.4 %copy-start.34 = (f32[1536]{0:T(1024)S(1)}, f32[1536]{0:T(1024)}, u32[]{:S(2)}) copy-start(f32[1536]{0:T(1024)} %param.20) | copy-start | bytes 18436
  92.6 4.6 %copy-start.13 = (f32[784,384]{1,0:T(8,128)S(1)}, f32[784,384]{1,0:T(8,128)}, u32[]{:S(2)}) copy-start(f32[784,384]{1,0:T(8,128)} %reshape.287) | copy-start | bytes 3612676
  92.6 4.6 %copy-start.33 = (bf16[1536,384]{1,0:T(8,128)(2,1)S(1)}, bf16[1536,384]{1,0:T(8,128)(2,1)}, u32[]{:S(2)}) copy-start(bf16[1536,384]{1,0:T(8,128)(2,1)} %param.21) | copy-start | bytes 3538948
  100.9 1.4 copy-start.10
  104.4 7.9 %copy-start.35 = (f32[384]{0:T(512)S(1)}, f32[384]{0:T(512)}, u32[]{:S(2)}) copy-start(f32[384]{0:T(512)} %param.22) | copy-start | bytes 4612
  106.1 26.2 %all-to-all-start.3 = ((bf16[32,7,7,384]{3,2,1,0:T(8,128)(2,1)}), bf16[32,7,7,384]{3,2,1,0:T(8,128)(2,1)}, u32[]{:S(2)}, u32[]{:S(2)}) async-start(bf16[32,7,7,384]{3,2,1,0:T(8,128)(2,1)} %copy.106), calls=%async_computation.3 | async-start | bytes 2752512 | tf_op jit(solution)/shard_map/all_to_all | solution.py:197
  112.3 330.5 %all-reduce.5.cloned.1.call-start = ((), (), s32[]{:S(2)}) async-start(), calls=%async_computation.4 | async-start | bytes 9609216 | tf_op jit(solution)/shard_map/psum | solution.py:224
  112.3 5.6 %copy-start.11 = (bf16[784,384]{1,0:T(8,128)(2,1)S(1)}, bf16[784,384]{1,0:T(8,128)(2,1)}, u32[]{:S(2)}) copy-start(bf16[784,384]{1,0:T(8,128)(2,1)} %reshape.282) | copy-start | bytes 1806340
  117.9 4.7 %copy-start.14 = (f32[784,384]{1,0:T(8,128)S(1)}, f32[784,384]{1,0:T(8,128)}, u32[]{:S(2)}) copy-start(f32[784,384]{1,0:T(8,128)} %reshape.287) | copy-start | bytes 3612676
  117.9 4.7 %copy-start.36 = (bf16[784,1536]{1,0:T(8,128)(2,1)S(1)}, bf16[784,1536]{1,0:T(8,128)(2,1)}, u32[]{:S(2)}) copy-start(bf16[784,1536]{1,0:T(8,128)(2,1)} %get-tuple-element.132) | copy-start | bytes 7225348
  122.6 9.7 %copy-start.23 = (s32[2,14]{1,0:T(2,128)S(1)}, s32[2,14]{1,0:T(2,128)}, u32[]{:S(2)}) copy-start(s32[2,14]{1,0:T(2,128)} %eq.76) | copy-start | bytes 340
  122.6 9.7 %copy-start.25 = (pred[2,14]{1,0:T(4,128)(4,1)S(1)}, pred[2,14]{1,0:T(4,128)(4,1)}, u32[]{:S(2)}) copy-start(pred[2,14]{1,0:T(4,128)(4,1)} %get-tuple-element.129) | copy-start | bytes 88
  140.5 2.8 copy-start.21
  143.3 3.3 copy-start.3
  143.3 3.6 copy-start.7
  155.2 5.5 %copy-start.6 = (bf16[14,98,384]{2,1,0:T(8,128)(2,1)S(1)}, bf16[14,98,384]{2,1,0:T(8,128)(2,1)}, u32[]{:S(2)}) copy-start(bf16[14,98,384]{2,1,0:T(8,128)(2,1)} %copy-done.4) | copy-start | bytes 3161092
  167.3 27.1 %all-to-all-start.1 = ((bf16[32,7,7,384]{3,2,1,0:T(8,128)(2,1)}), bf16[32,7,7,384]{3,2,1,0:T(8,128)(2,1)S(1)}, u32[]{:S(2)}, u32[]{:S(2)}) async-start(bf16[32,7,7,384]{3,2,1,0:T(8,128)(2,1)} %copy.98), calls=%async_computation.1 | async-start | bytes 2752512 | tf_op jit(solution)/shard_map/all_to_all | solution.py:196
  202.4 2.5 copy-start.26
  202.4 2.5 copy-start.29
  202.4 2.5 copy-start.32
  202.4 82.7 %copy-start.8 = (bf16[1,14,98,384]{3,2,1,0:T(8,128)(2,1)S(1)}, bf16[1,14,98,384]{3,2,1,0:T(8,128)(2,1)}, u32[]{:S(2)}) copy-start(bf16[1,14,98,384]{3,2,1,0:T(8,128)(2,1)} %param.12) | copy-start | bytes 3161092
  202.4 82.7 %copy-start.28 = (f32[384]{0:T(512)S(1)}, f32[384]{0:T(512)}, u32[]{:S(2)}) copy-start(f32[384]{0:T(512)} %param.23) | copy-start | bytes 4612
  444.3 3.4 copy-start.12
  444.3 4.8 %copy-start.1 = (bf16[384,1536]{1,0:T(8,128)(2,1)S(1)}, bf16[384,1536]{1,0:T(8,128)(2,1)}, u32[]{:S(2)}) copy-start(bf16[384,1536]{1,0:T(8,128)(2,1)} %param.19) | copy-start | bytes 3538948
Sparse Core Ops, SparseCore 0:
  165.3 277.3 all-reduce.4
where the time goes:
time: 458 us; the launch traced here: 456 us
  waiting for transfers between devices  197 us (43%)
  blocking collectives  80.2 us (18%)
  other arithmetic  51.8 us (11%)
  local copies, waits for them, and re-layouts  43.6 us (10%)
  matrix products  34.9 us (8%)
  starting transfers between devices  33.6 us (7%)
  between operations  15.1 us (3%)
    psum x1, waiting for transfers between devices, local(): lax.psum((grad_dw, grad_dwb, grad_gain, grad_lnb, grad_w1, grad_b1, grad_...  156 us
    psum x1, blocking collectives, local(): lax.psum((grad_dw, grad_dwb, grad_gain, grad_lnb, grad_w1, grad_b1, grad_...  80.2 us
    all_to_all x1, waiting for transfers between devices, local(): lax.all_to_all(back_branch, 'tile', split_axis=0, concat_axis=0, tiled=True)  21.4 us
    reduce_sum x1, other arithmetic, normalize(): mean_val = jnp.mean(conv_out, axis=-1, keepdims=True)  19.8 us
    reduce_sum x4, other arithmetic, conv_grad(): pieces.append(jnp.sum(window * grad_conv, axis=(0, 1)))  16.8 us
    all_to_all x1, waiting for transfers between devices, local(): lax.all_to_all(send_feat, 'tile', split_axis=0, concat_axis=0, tiled=True)  12.6 us
    unnamed x78, local copies, waits for them, and re-layouts  11.5 us
  transfers between devices with their start and end apart: 7, of which 4 were waited for; matrix products, arithmetic and copies ran while one was open for 15% of the time, Pallas kernels for 0%

commit v1 on v0

--- a/solution.py
+++ b/solution.py
@@ -132,76 +132,20 @@
     conv_out = depthwise(padded, dw_weight, dw_bias, height, breadth)
     centred, inv_std, normed_f = normalize(conv_out, ln_gain, ln_bias)
     normed = normed_f.astype(jnp.bfloat16)
-    cap = (tiles_here + ntile - 1) // ntile
-    slots_all = ntile * cap
-    target_dev = jnp.where(table >= 0, table // OWN, -1).reshape(ntile, tiles_here)
-    tile_ids = jnp.arange(tiles_here)
-    earlier = tile_ids[:, None] < tile_ids[None, :]
-    same_dev = target_dev[:, :, None] == target_dev[:, None, :]
-    order_in = jnp.sum((same_dev & earlier[None, :, :]).astype(jnp.int32), axis=1)
-    buffer_pos = target_dev * cap + order_in
-    my_pos = lax.dynamic_slice_in_dim(buffer_pos, my_index, 1, 0)[0]
-    buffer_ids = jnp.arange(slots_all)
-    flat_live = my_live.reshape(-1)
-    send_sel = (
-        ((buffer_ids[:, None] == my_pos[None, :]) & flat_live[None, :])
-        .astype(jnp.bfloat16)
-        .reshape(slots_all, rows_here, COLS)
-    )
-    send_feat = jnp.einsum(
-        "qrc,rpcvk->qpvk",
-        send_sel,
-        normed.reshape(rows_here, TP, COLS, TP, C),
-        preferred_element_type=jnp.bfloat16,
-    )
-    send_cot = jnp.einsum(
-        "qrc,rpcvk->qpvk",
-        send_sel,
-        slide_cot.reshape(rows_here, TP, COLS, TP, C),
-        preferred_element_type=jnp.bfloat16,
-    )
-    got_feat, got_cot = (
-        lax.all_to_all(send_feat, "tile", split_axis=0, concat_axis=0, tiled=True),
-        lax.all_to_all(send_cot, "tile", split_axis=0, concat_axis=0, tiled=True),
-    )
-    source_pos = jnp.arange(ntile)[:, None] * cap + order_in
-    for_me = (target_dev == my_index).reshape(-1, 1)
-    slot_hot = ((table.reshape(-1) % OWN)[:, None] == jnp.arange(OWN)[None, :]) & for_me
-    pos_hot = (source_pos.reshape(-1, 1) == buffer_ids[None, :]) & for_me
-    placing = contract_rows(slot_hot.astype(jnp.float32), pos_hot.astype(jnp.float32)).astype(
-        jnp.bfloat16
-    )
-    owned_feat = jnp.einsum(
-        "sq,qpvk->spvk", placing, got_feat, preferred_element_type=jnp.bfloat16
-    ).reshape(OWN * TP * TP, C)
-    owned_cot = jnp.einsum(
-        "sq,qpvk->spvk", placing, got_cot, preferred_element_type=jnp.bfloat16
-    ).reshape(OWN * TP * TP, C)
+    live_rows = tissue.reshape(height * breadth, 1)
     branch_rows, grad_rows, weight_grads = mlp_block(
-        owned_feat, owned_cot, 1.0, w_in, b_in, w_out, b_out, layer_scale, loss_scale
-    )
-    back_branch = jnp.einsum(
-        "sq,spvk->qpvk",
-        placing,
-        branch_rows.reshape(OWN, TP, TP, C),
-        preferred_element_type=jnp.bfloat16,
-    )
-    back_grad = jnp.einsum(
-        "sq,spvk->qpvk",
-        placing,
-        grad_rows.reshape(OWN, TP, TP, C),
-        preferred_element_type=jnp.bfloat16,
-    )
-    ret_branch, ret_grad = (
-        lax.all_to_all(back_branch, "tile", split_axis=0, concat_axis=0, tiled=True),
-        lax.all_to_all(back_grad, "tile", split_axis=0, concat_axis=0, tiled=True),
-    )
-    branch = jnp.einsum(
-        "qrc,qpvk->rpcvk", send_sel, ret_branch, preferred_element_type=jnp.bfloat16
-    ).reshape(height, breadth, C)
-    grad_xn = jnp.einsum(
-        "qrc,qpvk->rpcvk", send_sel, ret_grad, preferred_element_type=jnp.bfloat16
-    ).reshape(height, breadth, C)
+        normed.reshape(height * breadth, C),
+        slide_cot.reshape(height * breadth, C),
+        live_rows,
+        w_in,
+        b_in,
+        w_out,
+        b_out,
+        layer_scale,
+        loss_scale,
+    )
+    branch = branch_rows.reshape(height, breadth, C)
+    grad_xn = grad_rows.reshape(height, breadth, C)
     branch_f = branch.astype(jnp.float32)
     grad_xf = grad_xn.astype(jnp.float32)
     mixed = (tissue * (slide_feat.astype(jnp.float32) + layer_scale * branch_f)).astype(
@@ -221,21 +165,30 @@
     grad_dwb = jnp.sum(grad_conv, axis=(0, 1))
     grad_dw = conv_grad(padded, grad_conv, height, breadth)
     grad_w1, grad_b1, grad_w2, grad_b2 = weight_grads
-    summed = lax.psum(
-        (grad_dw, grad_dwb, grad_gain, grad_lnb, grad_w1, grad_b1, grad_w2, grad_b2, grad_scale),
-        ("slide", "tile"),
-    )
+    small = (grad_dw, grad_dwb, grad_gain, grad_lnb, grad_b1, grad_b2, grad_scale)
+    packed = jnp.concatenate([item.reshape(-1) for item in small]).reshape(-1, C)
+    large = jnp.concatenate([grad_w1.reshape(-1, C), grad_w2], axis=0).astype(jnp.bfloat16)
+    packed = lax.psum(packed, ("slide", "tile"))
+    large = lax.psum(large, ("slide", "tile")).astype(jnp.float32)
+    half = grad_w1.size // C
+    sums = []
+    start = 0
+    for item in small:
+        rows = item.size // C
+        sums.append(packed[start : start + rows].reshape(item.shape))
+        start += rows
+    dw, dwb, gain, lnb, b1, b2, scale = sums
     return (
         mixed[None],
-        summed[0],
-        summed[1],
-        summed[2],
-        summed[3],
-        summed[4],
-        summed[5],
-        summed[6],
-        summed[7],
-        summed[8],
+        dw,
+        dwb,
+        gain,
+        lnb,
+        large[:half].reshape(grad_w1.shape),
+        b1,
+        large[half:],
+        b2,
+        scale,
     )
 
 

time: 458 us -> 670 us (1.46)
  waiting for transfers between devices: 197 us -> 502 us
  blocking collectives: 80.2 us -> 0 us
  starting transfers between devices: 33.6 us -> 6.53 us
  local copies, waits for them, and re-layouts: 43.6 us -> 61.4 us
  matrix products: 34.9 us -> 25.2 us
    psum x1 -> x2, waiting for transfers between devices: 156 us -> 501 us  [the longest x1 258 us: local(): large = lax.psum(large, ('slide', 'tile')).astype(jnp.float32)]
    psum x1 -> x0, blocking collectives: 80.2 us -> none  [local(): lax.psum((grad_dw, grad_dwb, grad_gain, grad_lnb, grad_w1, grad_b1, grad_...]
    all_to_all x4 -> x0, waiting for transfers between devices: 40.6 us -> none  [the longest x1 21.4 us: local(): lax.all_to_all(back_branch, 'tile', split_axis=0, concat_axis=0, tiled=True)]
    all_to_all x4 -> x0, starting transfers between devices: 26.4 us -> none  [the longest x1 7.57 us: local(): lax.all_to_all(send_feat, 'tile', split_axis=0, concat_axis=0, tiled=True)]
    another operation x50, local copies, waits for them, and re-layouts: 0.35 us -> 22.1 us  [conv_grad(): return jnp.stack(pieces).reshape(K, K, -1)]
    dot_general x8 -> x0, matrix products: 12.2 us -> none  [the longest x1 3.65 us: local(): jnp.einsum('qrc,qpvk->rpcvk', send_sel, ret_grad, preferred_element_type=...]
  transfers between devices with their start and end apart: 7 -> 4, of which waited for: 4 -> 3; matrix products, arithmetic and copies ran while one was open for 15% -> 2% of each run, Pallas kernels for 0% -> 0%
where the time goes in v1:
time: 670 us; the launch traced here: 668 us
  waiting for transfers between devices  502 us (75%)
  local copies, waits for them, and re-layouts  61.4 us (9%)
  other arithmetic  58.4 us (9%)
  matrix products  25.2 us (4%)
  between operations  15.3 us (2%)
    psum x1, waiting for transfers between devices, local(): large = lax.psum(large, ('slide', 'tile')).astype(jnp.float32)  258 us
    psum x1, waiting for transfers between devices, local(): packed = lax.psum(packed, ('slide', 'tile'))  243 us
    reduce_sum x4, other arithmetic, conv_grad(): pieces.append(jnp.sum(window * grad_conv, axis=(0, 1)))  22.5 us
    another operation x50, local copies, waits for them, and re-layouts, conv_grad(): return jnp.stack(pieces).reshape(K, K, -1)  22.1 us
    reduce_sum x1, other arithmetic, normalize(): mean_val = jnp.mean(conv_out, axis=-1, keepdims=True)  19.8 us
  transfers between devices with their start and end apart: 4, of which 3 were waited for; matrix products, arithmetic and copies ran while one was open for 2% of the time, Pallas kernels for 0%

profile of v1, /device:TPU:1, one launch (start us, length us, event | category | flops | bytes accessed | tf_op | source)
XLA Modules:
  0.0 668.4 jit_solution(888725611247625686)
XLA Ops:
  7.3 0.9 constant_dynamic-slice_fusion
  8.7 1.5 bitcast_multiply_fusion.1
  10.3 1.0 copy-done.4
  11.3 4.5 collective-permute-start
  15.8 1.9 collective-permute-start.1
  17.8 0.7 slice_reduce_fusion.52
  18.5 0.7 slice_reduce_fusion.53
  19.2 0.7 slice_reduce_fusion.51
  19.8 0.8 mul.971
  20.6 1.5 reshape.154
  22.6 0.7 collective-permute-done.1
  23.3 2.0 fusion.114
  25.7 19.8 %fusion.121 = (f32[14,98]{1,0:T(8,128)S(1)}, f32[14,98,384]{2,1,0:T(8,128)S(1)}) fusion(f32[384]{0:T(512)} %get-tuple-element.119, bf16[20,104,384]{2,1,0:T(8,128)(2,1)S(1)} %fusion.114, f32[384]{0:T(512)} %get-tuple-element.120, f32[384]{0:T(512)S(1)} %copy-done.31, f32[384]{0:T(512)S(1)} %copy-done.32, bf16[3,98,384]{2,1,0:T(8,128)(2,1)S(1)} %collective-permute-done.1, ...), kind=kLoop, calls=%fused_computation.321 | loop fusion | flops 81133216 | bytes 47950192 | tf_op jit(solution)/shard_map/reduce_sum | solution.py:60
  46.1 0.8 copy-done.1
  46.8 1.5 add_convert_fusion
  48.3 2.3 reshape.141
  50.6 5.4 multiply_convert_fusion
  56.0 6.2 fusion.125
  62.1 3.1 convolution_convert_fusion.2
  65.3 4.3 fusion.120
  69.6 2.8 reshape.155
  72.4 3.2 multiply_reduce_fusion.1
  75.7 8.1 %fusion.105 = (f32[384]{0:T(512)S(1)}, f32[384]{0:T(512)S(1)}, f32[384]{0:T(512)S(1)}, f32[384]{0:T(512)S(1)}, f32[384]{0:T(512)S(1)}, /*index=5*/f32[384]{0:T(5...) fusion(bf16[20,104,384]{2,1,0:T(8,128)(2,1)S(1)} %fusion.114, ...), kind=kLoop, calls=%fused_computation.215 | loop fusion | flops 32130816 | bytes 25339840 | tf_op jit(solution)/shard_map/reduce_sum | solution.py:55
  83.8 6.3 fusion.84
  90.1 1.7 fusion.39
  91.9 3.8 convolution_convert_fusion.1
  95.7 2.4 fusion.7
  98.1 1.6 reshape.153
  99.8 1.6 reshape.157
  101.4 3.3 reshape.147
  104.7 1.2 stack.157
  105.9 1.3 stack.158
  107.2 1.2 stack.159
  108.4 1.3 stack.161
  109.6 1.3 stack.162
  110.9 1.2 stack.163
  112.1 1.3 stack.164
  113.4 1.2 stack.165
  114.6 1.3 stack.166
  115.9 1.2 stack.168
  117.1 1.3 stack.169
  118.4 1.2 stack.170
  119.6 1.2 stack.171
  123.7 6.4 fusion.102
  130.4 3.0 stack.199
  133.4 0.6 reshape_reshape.3
  134.0 4.0 multiply_reduce_fusion
  138.9 1.5 constant_dynamic-update-slice_fusion.6
  140.5 1.3 constant_dynamic-update-slice_fusion.5
  141.8 1.3 constant_dynamic-update-slice_fusion.4
  143.1 1.3 constant_dynamic-update-slice_fusion.3
  144.4 1.3 constant_dynamic-update-slice_fusion.2
  145.7 1.3 constant_dynamic-update-slice_fusion.1
  146.9 1.3 constant_dynamic-update-slice_fusion
  148.2 1.6 reshape.142
  149.8 1.6 pad_maximum_fusion
  151.5 243.1 %all-reduce.4.cloned.1.call-done = f32[58,384]{1,0:T(8,128)} async-done(((f32[58,384]{1,0:T(8,128)}), f32[58,384]{1,0:T(8,128)}) %all-reduce.4.cloned.1.call-update) | async-done | bytes 89104 | tf_op jit(solution)/shard_map/psum | solution.py:171
  394.6 0.9 slice.547
  395.5 0.6 reshape.143
  396.2 0.7 slice.552
  397.5 1.4 slice_reduce_fusion
  398.9 257.7 %all-reduce.6.cloned.1.call-done = bf16[3072,384]{1,0:T(8,128)(2,1)} async-done(((bf16[3072,384]{1,0:T(8,128)(2,1)}), bf16[3072,384]{1,0:T(8,128)(2,1)}) %all-reduce.6.cloned.1.call-update) | async-done | bytes 2359312 | tf_op jit(solution)/shard_map/psum | solution.py:172
  656.6 3.3 fusion.123
  660.0 1.6 reshape.148
  (199 shorter events, 6.0 us)
Async XLA Ops:
  7.2 43.4 %copy-start = (bf16[384,1536]{1,0:T(8,128)(2,1)S(1)}, bf16[384,1536]{1,0:T(8,128)(2,1)}, u32[]{:S(2)}) copy-start(bf16[384,1536]{1,0:T(8,128)(2,1)} %param.19) | copy-start | bytes 3538948
  7.2 10.6 %copy-start.17 = (f32[7,7,384]{2,1,0:T(8,128)S(1)}, f32[7,7,384]{2,1,0:T(8,128)}, u32[]{:S(2)}) copy-start(f32[7,7,384]{2,1,0:T(8,128)} %param.15) | copy-start | bytes 225796
  7.2 13.4 %copy-start.6 = (bf16[1,14,98,384]{3,2,1,0:T(8,128)(2,1)S(1)}, bf16[1,14,98,384]{3,2,1,0:T(8,128)(2,1)}, u32[]{:S(2)}) copy-start(bf16[1,14,98,384]{3,2,1,0:T(8,128)(2,1)} %param.13) | copy-start | bytes 3161092
  7.2 387.4 %all-reduce.4.cloned.1.call-start = ((), (), s32[]{:S(2)}) async-start(), calls=%async_computation | async-start | bytes 196608 | tf_op jit(solution)/shard_map/psum | solution.py:171
  11.3 10.9 %copy-start.19 = (f32[384]{0:T(512)S(1)}, f32[384]{0:T(512)}, u32[]{:S(2)}) copy-start(f32[384]{0:T(512)} %param.23) | copy-start | bytes 4612
  11.3 11.3 %collective-permute-start = (bf16[3,98,384]{2,1,0:T(8,128)(2,1)S(1)}, bf16[3,98,384]{2,1,0:T(8,128)(2,1)S(1)}, u32[]{:S(2)}, u32[]{:S(2)}) collective-permute-start(bf16[3,98,384]{2,1,0:T(8,128)(2,1)S(1)} %get-tuple-element.126), channel_id=1, source_target_pairs={{0,1},{1,2},{2,3},{3,4},{4,5},{5,6},{6,7},{7,8},{8,9},{9,10},{10,1... | collective-permute-start | bytes 677384 | tf_op jit(solution)/shard_map/ppermute | solution.py:20
  15.8 7.5 %collective-permute-start.1 = (bf16[3,98,384]{2,1,0:T(8,128)(2,1)S(1)}, bf16[3,98,384]{2,1,0:T(8,128)(2,1)S(1)}, u32[]{:S(2)}, u32[]{:S(2)}) collective-permute-start(bf16[3,98,384]{2,1,0:T(8,128)(2,1)S(1)} %get-tuple-element.127), channel_id=1, source_target_pairs={{1,0},{2,1},{3,2},{4,3},{5,4},{6,5},{7,6},{8,7},{9,8},{10,9},{11,1... | collective-permute-start | bytes 677384 | tf_op jit(solution)/shard_map/ppermute | solution.py:23
  22.2 3.1 copy-start.21
  22.2 3.1 copy-start.22
  22.2 3.1 copy-start.23
  22.2 3.1 copy-start.24
  22.2 3.1 copy-start.25
  22.2 3.1 copy-start.26
  22.3 3.1 copy-start.27
  22.3 3.1 copy-start.28
  22.3 3.1 copy-start.29
  22.3 3.1 copy-start.30
  22.3 3.1 copy-start.31
  22.3 3.1 copy-start.32
  22.3 3.1 copy-start.33
  22.3 3.1 copy-start.34
  22.3 3.1 copy-start.35
  22.3 3.1 copy-start.36
  22.4 3.1 copy-start.37
  22.4 3.1 copy-start.38
  22.4 3.1 copy-start.39
  22.4 3.1 copy-start.40
  22.4 3.1 copy-start.41
  22.4 3.1 copy-start.42
  22.4 3.1 copy-start.43
  22.4 3.1 copy-start.44
  22.4 3.1 copy-start.45
  22.4 3.1 copy-start.46
  22.5 3.1 copy-start.47
  22.5 3.1 copy-start.48
  22.5 3.1 copy-start.49
  22.5 3.1 copy-start.50
  22.5 3.1 copy-start.51
  22.5 3.1 copy-start.52
  22.5 3.1 copy-start.53
  22.5 3.1 copy-start.54
  22.5 3.1 copy-start.55
  22.6 22.8 %copy-start.10 = (bf16[3,98,384]{2,1,0:T(8,128)(2,1)}, bf16[3,98,384]{2,1,0:T(8,128)(2,1)S(1)}, u32[]{:S(2)}) copy-start(bf16[3,98,384]{2,1,0:T(8,128)(2,1)S(1)} %collective-permute-done) | copy-start | bytes 677380
  23.3 22.2 %copy-start.11 = (bf16[3,98,384]{2,1,0:T(8,128)(2,1)}, bf16[3,98,384]{2,1,0:T(8,128)(2,1)S(1)}, u32[]{:S(2)}) copy-start(bf16[3,98,384]{2,1,0:T(8,128)(2,1)S(1)} %collective-permute-done.1) | copy-start | bytes 677380
  46.8 3.7 copy-start.66
  50.6 5.4 copy-start.12
  50.6 5.4 copy-start.59
  50.6 5.4 copy-start.64
  56.0 6.2 copy-start.15
  75.7 16.2 %slice-start = ((s8[4227072]{0:T(1024)(128)(4,1)}), s8[4194304]{0:T(1024)(128)(4,1)S(1)}, s32[]{:S(2)}) async-start(s8[4227072]{0:T(1024)(128)(4,1)} %bitcast.20), calls=%async_computation.2 | async-start | bytes 8388608
  83.8 6.4 copy-start.2
  83.8 8.1 %slice-start.1 = ((s8[4227072]{0:T(1024)(128)(4,1)}), s8[32768]{0:T(1024)(128)(4,1)S(1)}, s32[]{:S(2)}) async-start(s8[4227072]{0:T(1024)(128)(4,1)} %bitcast.20), calls=%async_computation.3 | async-start | bytes 65536
  91.9 3.8 copy-start.65
  91.9 3.8 copy-start.67
  101.4 19.5 %copy-start.61 = (f32[384]{0:T(512)S(1)}, f32[384]{0:T(512)}, u32[]{:S(2)}) copy-start(f32[384]{0:T(512)} %get-tuple-element.34) | copy-start | bytes 4612
  101.4 20.0 %copy-start.60 = (f32[384]{0:T(512)S(1)}, f32[384]{0:T(512)}, u32[]{:S(2)}) copy-start(f32[384]{0:T(512)} %get-tuple-element.33) | copy-start | bytes 4612
  101.4 22.3 %copy-start.3 = (f32[14,98,384]{2,1,0:T(8,128)S(1)}, f32[14,98,384]{2,1,0:T(8,128)}, u32[]{:S(2)}) copy-start(f32[14,98,384]{2,1,0:T(8,128)} %copy-done.2) | copy-start | bytes 6322180
  134.0 4.1 copy-start.7
  134.0 4.1 copy-start.8
  138.1 5.0 copy-start.63
  138.1 6.3 copy-start.58
  138.1 11.7 %copy-start.9 = (bf16[1536,384]{1,0:T(8,128)(2,1)S(1)}, bf16[1536,384]{1,0:T(8,128)(2,1)}, u32[]{:S(2)}) copy-start(bf16[1536,384]{1,0:T(8,128)(2,1)} %reshape.147) | copy-start | bytes 3538948
  138.1 11.7 %copy-start.14 = (bf16[1536,384]{1,0:T(8,128)(2,1)S(1)}, bf16[1536,384]{1,0:T(8,128)(2,1)}, u32[]{:S(2)}) copy-start(bf16[1536,384]{1,0:T(8,128)(2,1)} %convolution_convert_fusion.1) | copy-start | bytes 3538948
  149.8 506.9 %all-reduce.6.cloned.1.call-start = ((), (), s32[]{:S(2)}) async-start(), calls=%async_computation.1 | async-start | bytes 4718592 | tf_op jit(solution)/shard_map/psum | solution.py:172
  (10 other events, 20.0 us)
Sparse Core Ops, SparseCore 0:
  149.9 244.7 all-reduce.3
  400.6 255.9 all-reduce.5
